TPU v7x, 128 devices: a whole 4x4x4 slice. The times are simulated.
128 devices in a mesh: row: 8 (over x, core), col: 16 (over z, y).
Axes of the slice: x: 4, y: 4, z: 4, core: 2. Of those that a mesh axis runs over, the one named last changes fastest.
Arguments:
- amplitudes: bfloat16 [1792, 23040], P('col', 'row'), may hold values from -6 to 6
- integrals: bfloat16 [23040, 23040], P('row', 'col'), may hold values from -0.026352314 to 0.026352314, as said below
- row_gap: float32 [1792], replicated, may hold values from 0.25 to 1
- col_gap: float32 [23040], replicated, may hold values from 0.25 to 1
Outputs:
- updated: bfloat16 [1792, 23040], P(None, ('row', 'col'))
Inputs may be any that keep to these rules, and one draw needn't show every extreme that they name: integrals is symmetric: entry (p, q) equals entry (q, p).
All inputs are finite; a program needn't handle non-finite values.
Results may differ from a plain program's by a relative error of at most 0.022.
Values may be sent and summed in bfloat16 or wider, within the bound.
A program may use at most 64 MiB of HBM per device.

v0:
```python
import functools

import jax
import jax.numpy as jnp
from jax import lax
from jax.experimental import pallas as pl
from jax.experimental.pallas import tpu as pltpu
from jax.sharding import PartitionSpec as P

MESH = pl.DeviceIdType.MESH
F32 = jnp.float32
BF16 = jnp.bfloat16

BLOCK = 16
SPLIT = 1408
WINDOW = 192
STRIDE = 176
TILE = 128
X_KIND = 14
RS_KIND = 24
KINDS = 40

PLAN = (
    ("r1", 8),
    ("r2", 10),
    ("a0", 0),
    ("m1", 3),
    ("b2", 4),
    ("b4", 5),
    ("r3", 12),
    ("a3", 2),
    ("a2", 1),
    ("r4", 14),
    ("sw", 14),
    ("tv", 0),
    ("a1", 0),
    ("m2", 6),
    ("b1", 3),
    ("b3", 4),
    ("b5", 5),
)


def kernel(
    a_ref, vt_hbm, row_hbm, col_ref, o_ref, final_ref,
    rg, near, cg, v, stage, turned, ag, c1, cx, xo, xn, sg, w, ro1, rn1, ro2, rn2, out, gsem, lsem, send, recv,
):
    chunks = ag.shape[0]
    depth, width = a_ref.shape[1], v.shape[1]
    group = depth // 4
    row, col = lax.axis_index("row"), lax.axis_index("col")
    x, core = row // 2, row % 2
    z, y = col // 4, col % 4
    half = core * 128
    other = 128 - half

    def around(index):
        return {0: index, 1: lax.rem(index + 1, 4), 2: lax.rem(index + 2, 4), -1: lax.rem(index + 3, 4)}

    xs, ys, zs = around(x), around(y), around(z)
    at = {"z": zs, "y": ys}
    peer = {
        ("x", 1): (xs[1] * 2 + core, col),
        ("x", -1): (xs[-1] * 2 + core, col),
        ("y", 1): (row, z * 4 + ys[1]),
        ("y", -1): (row, z * 4 + ys[-1]),
        ("z", 1): (row, zs[1] * 4 + y),
        ("z", -1): (row, zs[-1] * 4 + y),
        "core": (x * 2 + 1 - core, col),
    }
    strips = {step: half + index * 32 for step, index in xs.items()}
    gather = (("y", "z", pl.ds(0, SPLIT)), ("z", "y", pl.ds(SPLIT, ag.shape[-1] - SPLIT)))
    scatter = (("z", "y"), ("y", "z"))

    def copy(c, kind, src, dst, to):
        return pltpu.make_async_remote_copy(
            src_ref=src, dst_ref=dst, send_sem=send.at[c, kind], recv_sem=recv.at[c, kind],
            device_id=to, device_id_type=MESH,
        )

    def arrived(c, kind, dst):
        copy(c, kind, dst, dst, peer["core"]).wait_recv()

    def sent(c, kind, src):
        copy(c, kind, src, src, peer["core"]).wait_send()

    def block(s, c, step):
        first, _, lanes = gather[s]
        f = at[first][step]
        return ag.at[c, z, f, :, lanes] if first == "y" else ag.at[c, f, y, :, lanes]

    def line(s, c, step, start=0, size=4):
        first, second, lanes = gather[s]
        g, part = at[second][step], pl.ds(start, size)
        return ag.at[c, g, part, :, lanes] if first == "y" else ag.at[c, part, g, :, lanes]

    def a_send(c, s, k, d=1):
        first, second, _ = gather[s]
        if k == 0:
            return block(s, c, 0), peer[first, 1]
        if k == 1:
            return block(s, c, 0), peer[first, -1]
        if k == 2:
            return block(s, c, -d), peer[first, d]
        if k == 3:
            return line(s, c, 0), peer[second, 1]
        if k == 4:
            return line(s, c, 0), peer[second, -1]
        if k == 5:
            return line(s, c, -1, 0, 2), peer[second, 1]
        return line(s, c, 1, 2, 2), peer[second, -1]

    def a_land(c, s, k):
        if k < 3:
            return block(s, c, (-1, 1, 2)[k])
        if k < 5:
            return line(s, c, (-1, 1)[k - 3])
        return line(s, c, 2, 2 * (k - 5), 2)

    def a_start(c, s, k, d=1):
        src, to = a_send(c, s, k, d)
        copy(c, s * 7 + k, src, src, to).start()

    def a_wait(c, s, k):
        arrived(c, s * 7 + k, a_land(c, s, k))

    def a0(c):
        for s in range(2):
            a_start(c, s, 0)
            a_start(c, s, 1)

    def a1(c):
        def forward(d):
            for s in range(2):
                a_wait(c, s, 0 if d == 1 else 1)
                a_start(c, s, 2, d)

        pl.when(c % 2 == 0)(lambda: forward(1))
        pl.when(c % 2 == 1)(lambda: forward(-1))

    def a2(c):
        pl.when(c % 2 == 0)(lambda: [a_wait(c, s, 1) for s in range(2)] and None)
        pl.when(c % 2 == 1)(lambda: [a_wait(c, s, 0) for s in range(2)] and None)
        for s in range(2):
            a_wait(c, s, 2)
            a_start(c, s, 3)
            a_start(c, s, 4)

    def a3(c):
        for s in range(2):
            a_wait(c, s, 3)
            a_start(c, s, 5)
            a_wait(c, s, 4)
            a_start(c, s, 6)

    def m1(c):
        for s in range(2):
            a_wait(c, s, 5)
            a_wait(c, s, 6)
        rows = ag[c].reshape(16 * BLOCK, ag.shape[-1])
        for lo in range(0, width, 512):
            hi = min(lo + 512, width)
            c1[c, :, lo:hi] = jnp.dot(rows, v[:, lo:hi], preferred_element_type=F32).astype(BF16)
        x_start(c, 0)

    def piece(step, start=0, size=32):
        return pl.ds(pl.multiple_of(strips[step] + start, 16), size)

    def x_send(c, k):
        if k == 0:
            return c1.at[c, pl.ds(pl.multiple_of(other, 128), 128)], cx.at[c], peer["core"]
        if k == 9:
            src = sg.at[c, pl.ds(pl.multiple_of(half, 128), 128)]
            return src, src, peer["core"]
        d = 1 if k % 2 == 1 else -1
        part = pl.ds(8 - 8 * d, 16)
        if k < 3:
            return c1.at[c, piece(2, 8 - 8 * d, 16)], xo.at[c, part], peer["x", d]
        if k < 5:
            return c1.at[c, piece(d)], xn.at[c, (k - 3)], peer["x", d]
        src = sg.at[c, piece(0) if k < 7 else piece(-d, 8 - 8 * d, 16)]
        return src, src, peer["x", d]

    def x_land(c, k):
        if k < 5:
            return x_send(c, k)[1]
        if k == 9:
            return sg.at[c, pl.ds(pl.multiple_of(other, 128), 128)]
        d = 1 if k % 2 == 1 else -1
        return sg.at[c, piece(-d) if k < 7 else piece(2, 8 - 8 * d, 16)]

    def x_start(c, k):
        src, dst, to = x_send(c, k)
        copy(c, X_KIND + k, src, dst, to).start()

    def x_wait(c, k):
        arrived(c, X_KIND + k, x_land(c, k))

    def b1(c):
        x_wait(c, 0)
        rows = pl.ds(pl.multiple_of(half, 128), 128)
        c1[c, rows, :] = (c1[c, rows, :].astype(F32) + cx[c].astype(F32)).astype(BF16)
        x_start(c, 1)
        x_start(c, 2)

    def b2(c):
        for k, step in ((1, 1), (2, -1)):
            x_wait(c, k)
            part, rows = pl.ds(16 * (k - 1), 16), piece(step, 16 * (k - 1), 16)
            c1[c, rows, :] = (c1[c, rows, :].astype(F32) + xo[c, part].astype(F32)).astype(BF16)
            x_start(c, k + 2)

    first_row = (core * 8 + x * 2) * (chunks * BLOCK)

    def b3(c):
        gap = jnp.zeros((32, 128), F32)
        index = lax.broadcasted_iota(jnp.int32, (32, 128), 0)
        for k in range(32):
            value = rg[first_row + (k // BLOCK) * (chunks * BLOCK) + c * BLOCK + k % BLOCK]
            gap = jnp.where(index == k, value, gap)
        x_wait(c, 3)
        x_wait(c, 4)
        rows = piece(0)
        total = c1[c, rows, :].astype(F32) + xn[c, 0].astype(F32) + xn[c, 1].astype(F32)
        sg[c, rows, :] = (total / (gap[:, :1] + cg[0:1, :width])).astype(BF16)
        x_start(c, 5)
        x_start(c, 6)

    def b4(c):
        for k in (5, 6):
            x_wait(c, k)
            x_start(c, k + 2)

    def b5(c):
        x_wait(c, 7)
        x_wait(c, 8)
        x_start(c, 9)

    def r_move(c, s, k):
        first, second = scatter[s]
        fs, gs = at[first], at[second]
        d = 1 if k % 2 == 0 else -1
        if k < 2:
            part = pl.ds(2 * k, 2)
            return w.at[s, c, fs[2], part], ro1.at[s, c, part], peer[first, d]
        if k < 4:
            return w.at[s, c, fs[d]], rn1.at[s, c, k - 2], peer[first, d]
        if k < 6:
            part = pl.ds((k - 4) * (WINDOW // 2), WINDOW // 2)
            return w.at[s, c, fs[0], gs[2], part], ro2.at[s, c, part], peer[second, d]
        return w.at[s, c, fs[0], gs[d]], rn2.at[s, c, k - 6], peer[second, d]

    def r_start(c, s, k):
        src, dst, to = r_move(c, s, k)
        copy(c, RS_KIND + s * 8 + k, src, dst, to).start()

    def r_wait(c, s, k):
        arrived(c, RS_KIND + s * 8 + k, r_move(c, s, k)[1])

    def m2(c):
        x_wait(c, 9)

        turned[...] = sg[c].T

        def rows_of(q, carry):
            part = jnp.dot(
                v[pl.ds(pl.multiple_of(q * group, 16), group), :], turned[...], preferred_element_type=F32
            ).astype(BF16)
            for p in range(4):
                piece = part[p * STRIDE : p * STRIDE + WINDOW]
                w[0, c, q, p] = piece[:, :128]
                w[1, c, p, q] = piece[:, 128:]
            return carry

        lax.fori_loop(0, 4, rows_of, 0)
        for s in range(2):
            r_start(c, s, 0)
            r_start(c, s, 1)

    def r1(c):
        for s in range(2):
            up, down = at[scatter[s][0]][1], at[scatter[s][0]][-1]
            r_wait(c, s, 0)
            w[s, c, up, 0:2] = (w[s, c, up, 0:2].astype(F32) + ro1[s, c, 0:2].astype(F32)).astype(BF16)
            r_start(c, s, 2)
            r_wait(c, s, 1)
            w[s, c, down, 2:4] = (w[s, c, down, 2:4].astype(F32) + ro1[s, c, 2:4].astype(F32)).astype(BF16)
            r_start(c, s, 3)

    def r2(c):
        for s in range(2):
            f = at[scatter[s][0]][0]
            r_wait(c, s, 2)
            r_wait(c, s, 3)
            total = w[s, c, f].astype(F32) + rn1[s, c, 0].astype(F32) + rn1[s, c, 1].astype(F32)
            w[s, c, f] = total.astype(BF16)
            r_start(c, s, 4)
            r_start(c, s, 5)

    def r3(c):
        h = WINDOW // 2
        for s in range(2):
            f, gs = at[scatter[s][0]][0], at[scatter[s][1]]
            up, down = gs[1], gs[-1]
            r_wait(c, s, 4)
            w[s, c, f, up, :h] = (w[s, c, f, up, :h].astype(F32) + ro2[s, c, :h].astype(F32)).astype(BF16)
            r_start(c, s, 6)
            r_wait(c, s, 5)
            w[s, c, f, down, h:] = (w[s, c, f, down, h:].astype(F32) + ro2[s, c, h:].astype(F32)).astype(BF16)
            r_start(c, s, 7)

    def r4(c):
        sums = []
        for s in range(2):
            f, g = at[scatter[s][0]][0], at[scatter[s][1]][0]
            r_wait(c, s, 6)
            r_wait(c, s, 7)
            sums.append(w[s, c, f, g].astype(F32) + rn2[s, c, 0].astype(F32) + rn2[s, c, 1].astype(F32))
        total = jnp.concatenate(sums, axis=1)
        total = jnp.concatenate([total, jnp.zeros((256 - WINDOW, 256), F32)], axis=0)
        total = pltpu.roll(total, (256 - 4 * y) % 256, 0)
        out[:, c] = total.T.reshape(16, BLOCK, 256)

    def sw(c):
        for s in range(2):
            for k in range(7):
                sent(c, s * 7 + k, a_send(c, s, k)[0])
            for k in range(8):
                sent(c, RS_KIND + s * 8 + k, r_move(c, s, k)[0])
        for k in range(10):
            sent(c, X_KIND + k, x_send(c, k)[0])

    def load(i, size):
        slot = i % 2
        return pltpu.make_async_copy(
            vt_hbm.at[pl.ds(pl.multiple_of(i * TILE, TILE), size)], stage.at[slot, pl.ds(0, size)], lsem.at[slot]
        )

    tiles, rest = width // TILE, width % TILE
    third = (tiles + 1) // 3

    def tv(c):
        def turn(i, carry):
            load(i, TILE).wait()
            v[:depth, pl.ds(pl.multiple_of(i * TILE, TILE), TILE)] = stage[i % 2].T
            pl.when(i + 2 < tiles)(lambda: load(i + 2, TILE).start())
            pl.when(i + 2 == tiles)(lambda: load(tiles, rest).start())
            return carry

        lax.fori_loop(c * third, jnp.minimum((c + 1) * third, tiles), turn, 0)

        @pl.when(c == 2)
        def _():
            load(tiles, rest).wait()
            v[:depth, tiles * TILE :] = stage[tiles % 2, :rest].T

    load(0, TILE).start()
    load(1, TILE).start()
    rows_gap = pltpu.make_async_copy(row_hbm, rg, gsem)
    rows_gap.start()
    v[depth:, :] = jnp.zeros((v.shape[0] - depth, width), BF16)
    for c in range(chunks):
        ag[c, z, y, :, :depth] = a_ref[c * BLOCK : (c + 1) * BLOCK, :]
        ag[c, z, y, :, depth:] = jnp.zeros((BLOCK, ag.shape[-1] - depth), BF16)

    barrier = pltpu.get_barrier_semaphore()
    for to in peer.values():
        pl.semaphore_signal(barrier, inc=1, device_id=to, device_id_type=MESH)
    pl.semaphore_wait(barrier, len(peer))

    final = final_ref.shape[-1]
    inner, outer = col * width, (row * 16 + col) * final
    inner_row = inner // 128
    outer_row = jnp.minimum(outer // 128, col_ref.shape[0] - 3)
    for k in range(12):
        near[:, 128 * k : 128 * (k + 1)] = col_ref[pl.ds(inner_row + k, 1), :]
    for k in range(3):
        near[:, 1536 + 128 * k : 1664 + 128 * k] = col_ref[pl.ds(outer_row + k, 1), :]
    cg[...] = pltpu.roll(jnp.broadcast_to(near[:, :1536], (8, 1536)), (1536 - (inner - inner_row * 128)) % 1536, 1)
    shifted = pltpu.roll(jnp.broadcast_to(near[:, 1536:], (8, 384)), (384 - (outer - outer_row * 128)) % 384, 1)
    final_ref[...] = shifted[0:1, :final]
    rows_gap.wait()

    ops = dict(tv=tv, a0=a0, a1=a1, a2=a2, a3=a3, m1=m1, b1=b1, b2=b2, b3=b3, b4=b4, b5=b5, m2=m2, r1=r1, r2=r2, r3=r3, r4=r4, sw=sw)

    def step(t, carry):
        for name, late in PLAN:
            c = t - late
            pl.when(jnp.logical_and(c >= 0, c < (3 if name == "tv" else chunks)))(functools.partial(ops[name], c))
        return carry

    lax.fori_loop(0, chunks + max(late for _, late in PLAN), step, 0)
    for k in range(chunks):
        lanes = pl.ds(k * 256, 256)
        rows = out.reshape(16 * chunks * BLOCK, 256)[lanes, :]
        o_ref[:, lanes] = rows.T[:final]


def on_device(amplitudes, integrals, row_gap, col_gap):
    rows, depth = amplitudes.shape
    width = integrals.shape[1]
    chunks = rows // BLOCK
    final = depth // 16
    padded = (depth + 127) // 128 * 128

    vm = pl.BlockSpec(memory_space=pltpu.VMEM)
    anywhere = pl.BlockSpec(memory_space=pl.ANY)
    cycle_two, here = pl.pallas_call(
        kernel,
        out_shape=(
            jax.ShapeDtypeStruct((final, 16 * rows), F32),
            jax.ShapeDtypeStruct((1, final), F32),
        ),
        in_specs=[vm, anywhere, anywhere, vm],
        out_specs=(vm, vm),
        scratch_shapes=[
            pltpu.SMEM((16 * rows,), F32),
            pltpu.VMEM((1, 1920), F32),
            pltpu.VMEM((8, 1536), F32),
            pltpu.VMEM((padded, width), BF16),
            pltpu.VMEM((2, TILE, depth), BF16),
            pltpu.VMEM((width, 256), BF16),
            pltpu.VMEM((chunks, 4, 4, BLOCK, padded), BF16),
            pltpu.VMEM((chunks, 256, width), BF16),
            pltpu.VMEM((chunks, 128, width), BF16),
            pltpu.VMEM((chunks, 32, width), BF16),
            pltpu.VMEM((chunks, 2, 32, width), BF16),
            pltpu.VMEM((chunks, 256, width), BF16),
            pltpu.VMEM((2, chunks, 4, 4, WINDOW, 128), BF16),
            pltpu.VMEM((2, chunks, 4, WINDOW, 128), BF16),
            pltpu.VMEM((2, chunks, 2, 4, WINDOW, 128), BF16),
            pltpu.VMEM((2, chunks, WINDOW, 128), BF16),
            pltpu.VMEM((2, chunks, 2, WINDOW, 128), BF16),
            pltpu.VMEM((16, chunks, BLOCK, 256), F32),
            pltpu.SemaphoreType.DMA,
            pltpu.SemaphoreType.DMA((2,)),
            pltpu.SemaphoreType.DMA((chunks, KINDS)),
            pltpu.SemaphoreType.DMA((chunks, KINDS)),
        ],
        compiler_params=pltpu.CompilerParams(
            collective_id=0, has_side_effects=True, vmem_limit_bytes=62 * 1024 * 1024
        ),
        cost_estimate=pl.CostEstimate(
            flops=4 * 16 * rows * depth * width, bytes_accessed=2 * depth * width, transcendentals=0
        ),
    )(amplitudes, integrals.T, row_gap, col_gap.reshape(-1, 128))
    return (cycle_two.T / (row_gap[:, None] + here)).astype(BF16)


def solution(mesh):
    return jax.shard_map(
        on_device,
        mesh=mesh,
        in_specs=(P("col", "row"), P("row", "col"), P(), P()),
        out_specs=P(None, ("row", "col")),
        check_vma=False,
    )
```

profile of v0, /device:TPU:0, one launch (start us, length us, event | category | flops | bytes accessed | tf_op | source)
XLA Modules:
  0.0 141.8 jit_solution(376885412257181482)
XLA Ops:
  0.0 0.0 copy-start
  0.0 139.4 %shard_map.46 = (f32[180,1792]{1,0:T(8,128)}, f32[1,180]{1,0:T(1,128)}) custom-call(bf16[112,2880]{1,0:T(8,128)(2,1)} %a_ref.1, bf16[1440,2880]{1,0:T(8,128)(2,1)} %bitcast.8, f32[1792]{0:T(1024)} %row_hbm.1, f32[180,128]{1,0:T(8,128)} %bitcast.9), custom_call_target="tpu_custom_call" | custom-call | flops 29727129600 | bytes 8294400 | tf_op jit(solution)/shard_map/pallas_call | solution.py:408
  139.4 0.0 copy-done
  139.4 2.4 %fusion = bf16[1792,180]{0,1:T(8,128)(2,1)} fusion(f32[180,1792]{1,0:T(8,128)} %get-tuple-element.7, f32[180]{0:T(256)} %bitcast.7, f32[1792]{0:T(1024)S(1)} %copy-done), kind=kLoop, calls=%fused_computation.1 | loop fusion | flops 967680 | bytes 1943248 | tf_op jit(solution)/shard_map/convert_element_type | solution.py:447
Async XLA Ops:
  0.0 139.4 %copy-start = (f32[1792]{0:T(1024)S(1)}, f32[1792]{0:T(1024)}, u32[]{:S(2)}) copy-start(f32[1792]{0:T(1024)} %row_hbm.1) | copy-start | bytes 21508
where the time goes:
time: 142 us
  Pallas kernels  139 us (98%)
  other arithmetic  2.41 us (2%)
    pallas_call x1, Pallas kernels, on_device(): pl.pallas_call(kernel, out_shape=(jax.ShapeDtypeStruct((final, 16 * rows)...  139 us

commit v1 on v0

--- a/solution.py
+++ b/solution.py
@@ -16,6 +16,8 @@
 WINDOW = 192
 STRIDE = 176
 TILE = 128
+CUT = 368
+SLOTS = 4
 X_KIND = 14
 RS_KIND = 24
 KINDS = 40
@@ -24,6 +26,7 @@
     ("r1", 8),
     ("r2", 10),
     ("a0", 0),
+    ("cw", 7),
     ("m1", 3),
     ("b2", 4),
     ("b4", 5),
@@ -42,12 +45,12 @@
 
 
 def kernel(
-    a_ref, vt_hbm, row_hbm, col_ref, o_ref, final_ref,
-    rg, near, cg, v, stage, turned, ag, c1, cx, xo, xn, sg, w, ro1, rn1, ro2, rn2, out, gsem, lsem, send, recv,
+    a_ref, vt_hbm, row_ref, col_ref, o_ref,
+    near, cg, cf, rc, v, stage, turned, ag, c1, cx, xo, xn, sg, wq, w1, w2, ro1, rn1, ro2, rn2, out, lsem, send, recv,
 ):
     chunks = ag.shape[0]
     depth, width = a_ref.shape[1], v.shape[1]
-    group = depth // 4
+    group, final = depth // 4, o_ref.shape[0]
     row, col = lax.axis_index("row"), lax.axis_index("col")
     x, core = row // 2, row % 2
     z, y = col // 4, col % 4
@@ -160,7 +163,7 @@
         rows = ag[c].reshape(16 * BLOCK, ag.shape[-1])
         for lo in range(0, width, 512):
             hi = min(lo + 512, width)
-            c1[c, :, lo:hi] = jnp.dot(rows, v[:, lo:hi], preferred_element_type=F32).astype(BF16)
+            c1[c % SLOTS, :, lo:hi] = jnp.dot(rows, v[:, lo:hi], preferred_element_type=F32).astype(BF16)
         x_start(c, 0)
 
     def piece(step, start=0, size=32):
@@ -168,16 +171,16 @@
 
     def x_send(c, k):
         if k == 0:
-            return c1.at[c, pl.ds(pl.multiple_of(other, 128), 128)], cx.at[c], peer["core"]
+            return c1.at[c % SLOTS, pl.ds(pl.multiple_of(other, 128), 128)], cx.at[c], peer["core"]
         if k == 9:
             src = sg.at[c, pl.ds(pl.multiple_of(half, 128), 128)]
             return src, src, peer["core"]
         d = 1 if k % 2 == 1 else -1
         part = pl.ds(8 - 8 * d, 16)
         if k < 3:
-            return c1.at[c, piece(2, 8 - 8 * d, 16)], xo.at[c, part], peer["x", d]
+            return c1.at[c % SLOTS, piece(2, 8 - 8 * d, 16)], xo.at[c, part], peer["x", d]
         if k < 5:
-            return c1.at[c, piece(d)], xn.at[c, (k - 3)], peer["x", d]
+            return c1.at[c % SLOTS, piece(d)], xn.at[c, (k - 3)], peer["x", d]
         src = sg.at[c, piece(0) if k < 7 else piece(-d, 8 - 8 * d, 16)]
         return src, src, peer["x", d]
 
@@ -199,7 +202,7 @@
     def b1(c):
         x_wait(c, 0)
         rows = pl.ds(pl.multiple_of(half, 128), 128)
-        c1[c, rows, :] = (c1[c, rows, :].astype(F32) + cx[c].astype(F32)).astype(BF16)
+        c1[c % SLOTS, rows, :] = (c1[c % SLOTS, rows, :].astype(F32) + cx[c].astype(F32)).astype(BF16)
         x_start(c, 1)
         x_start(c, 2)
 
@@ -207,21 +210,15 @@
         for k, step in ((1, 1), (2, -1)):
             x_wait(c, k)
             part, rows = pl.ds(16 * (k - 1), 16), piece(step, 16 * (k - 1), 16)
-            c1[c, rows, :] = (c1[c, rows, :].astype(F32) + xo[c, part].astype(F32)).astype(BF16)
+            c1[c % SLOTS, rows, :] = (c1[c % SLOTS, rows, :].astype(F32) + xo[c, part].astype(F32)).astype(BF16)
             x_start(c, k + 2)
 
-    first_row = (core * 8 + x * 2) * (chunks * BLOCK)
-
     def b3(c):
-        gap = jnp.zeros((32, 128), F32)
-        index = lax.broadcasted_iota(jnp.int32, (32, 128), 0)
-        for k in range(32):
-            value = rg[first_row + (k // BLOCK) * (chunks * BLOCK) + c * BLOCK + k % BLOCK]
-            gap = jnp.where(index == k, value, gap)
+        gap = rc[pl.ds(core * 8 + x * 2, 2), c].reshape(32, 128)
         x_wait(c, 3)
         x_wait(c, 4)
         rows = piece(0)
-        total = c1[c, rows, :].astype(F32) + xn[c, 0].astype(F32) + xn[c, 1].astype(F32)
+        total = c1[c % SLOTS, rows, :].astype(F32) + xn[c, 0].astype(F32) + xn[c, 1].astype(F32)
         sg[c, rows, :] = (total / (gap[:, :1] + cg[0:1, :width])).astype(BF16)
         x_start(c, 5)
         x_start(c, 6)
@@ -241,14 +238,14 @@
         fs, gs = at[first], at[second]
         d = 1 if k % 2 == 0 else -1
         if k < 2:
-            part = pl.ds(2 * k, 2)
-            return w.at[s, c, fs[2], part], ro1.at[s, c, part], peer[first, d]
+            part = pl.ds(0, CUT) if k == 0 else pl.ds(CUT, group - CUT)
+            return w1.at[s, c, fs[2], part], ro1.at[s, c, part], peer[first, d]
         if k < 4:
-            return w.at[s, c, fs[d]], rn1.at[s, c, k - 2], peer[first, d]
+            return w1.at[s, c, fs[d]], rn1.at[s, c, k - 2], peer[first, d]
         if k < 6:
             part = pl.ds((k - 4) * (WINDOW // 2), WINDOW // 2)
-            return w.at[s, c, fs[0], gs[2], part], ro2.at[s, c, part], peer[second, d]
-        return w.at[s, c, fs[0], gs[d]], rn2.at[s, c, k - 6], peer[second, d]
+            return w2.at[s, c, gs[2], part], ro2.at[s, c, part], peer[second, d]
+        return w2.at[s, c, gs[d]], rn2.at[s, c, k - 6], peer[second, d]
 
     def r_start(c, s, k):
         src, dst, to = r_move(c, s, k)
@@ -262,17 +259,13 @@
 
         turned[...] = sg[c].T
 
-        def rows_of(q, carry):
-            part = jnp.dot(
-                v[pl.ds(pl.multiple_of(q * group, 16), group), :], turned[...], preferred_element_type=F32
-            ).astype(BF16)
+        for q in range(4):
+            part = jnp.dot(v[q * group : (q + 1) * group, :], turned[...], preferred_element_type=F32)
+            w1[0, c, q] = part[:, :128].astype(BF16)
             for p in range(4):
-                piece = part[p * STRIDE : p * STRIDE + WINDOW]
-                w[0, c, q, p] = piece[:, :128]
-                w[1, c, p, q] = piece[:, 128:]
-            return carry
-
-        lax.fori_loop(0, 4, rows_of, 0)
+                wq[p, q * final : (q + 1) * final] = part[p * final : (p + 1) * final, 128:]
+        for p in range(4):
+            w1[1, c, p] = wq[p].astype(BF16)
         for s in range(2):
             r_start(c, s, 0)
             r_start(c, s, 1)
@@ -281,10 +274,10 @@
         for s in range(2):
             up, down = at[scatter[s][0]][1], at[scatter[s][0]][-1]
             r_wait(c, s, 0)
-            w[s, c, up, 0:2] = (w[s, c, up, 0:2].astype(F32) + ro1[s, c, 0:2].astype(F32)).astype(BF16)
+            w1[s, c, up, :CUT] = (w1[s, c, up, :CUT].astype(F32) + ro1[s, c, :CUT].astype(F32)).astype(BF16)
             r_start(c, s, 2)
             r_wait(c, s, 1)
-            w[s, c, down, 2:4] = (w[s, c, down, 2:4].astype(F32) + ro1[s, c, 2:4].astype(F32)).astype(BF16)
+            w1[s, c, down, CUT:] = (w1[s, c, down, CUT:].astype(F32) + ro1[s, c, CUT:].astype(F32)).astype(BF16)
             r_start(c, s, 3)
 
     def r2(c):
@@ -292,34 +285,41 @@
             f = at[scatter[s][0]][0]
             r_wait(c, s, 2)
             r_wait(c, s, 3)
-            total = w[s, c, f].astype(F32) + rn1[s, c, 0].astype(F32) + rn1[s, c, 1].astype(F32)
-            w[s, c, f] = total.astype(BF16)
+            total = w1[s, c, f].astype(F32) + rn1[s, c, 0].astype(F32) + rn1[s, c, 1].astype(F32)
+            total = total.astype(BF16)
+            for p in range(4):
+                w2[s, c, p] = total[p * STRIDE : p * STRIDE + WINDOW]
             r_start(c, s, 4)
             r_start(c, s, 5)
 
     def r3(c):
         h = WINDOW // 2
         for s in range(2):
-            f, gs = at[scatter[s][0]][0], at[scatter[s][1]]
-            up, down = gs[1], gs[-1]
+            up, down = at[scatter[s][1]][1], at[scatter[s][1]][-1]
             r_wait(c, s, 4)
-            w[s, c, f, up, :h] = (w[s, c, f, up, :h].astype(F32) + ro2[s, c, :h].astype(F32)).astype(BF16)
+            w2[s, c, up, :h] = (w2[s, c, up, :h].astype(F32) + ro2[s, c, :h].astype(F32)).astype(BF16)
             r_start(c, s, 6)
             r_wait(c, s, 5)
-            w[s, c, f, down, h:] = (w[s, c, f, down, h:].astype(F32) + ro2[s, c, h:].astype(F32)).astype(BF16)
+            w2[s, c, down, h:] = (w2[s, c, down, h:].astype(F32) + ro2[s, c, h:].astype(F32)).astype(BF16)
             r_start(c, s, 7)
 
     def r4(c):
         sums = []
         for s in range(2):
-            f, g = at[scatter[s][0]][0], at[scatter[s][1]][0]
+            g = at[scatter[s][1]][0]
             r_wait(c, s, 6)
             r_wait(c, s, 7)
-            sums.append(w[s, c, f, g].astype(F32) + rn2[s, c, 0].astype(F32) + rn2[s, c, 1].astype(F32))
+            total = w2[s, c, g].astype(F32) + rn2[s, c, 0].astype(F32) + rn2[s, c, 1].astype(F32)
+            sums.append(pltpu.roll(total, lax.rem(WINDOW - 4 * g, WINDOW), 0))
         total = jnp.concatenate(sums, axis=1)
         total = jnp.concatenate([total, jnp.zeros((256 - WINDOW, 256), F32)], axis=0)
-        total = pltpu.roll(total, (256 - 4 * y) % 256, 0)
-        out[:, c] = total.T.reshape(16, BLOCK, 256)
+        gap = rc[:, c].reshape(256, 128)
+        gap = jnp.concatenate([gap, gap], axis=1) + cf[0:1, :]
+        out[:, c] = (total.T / gap).astype(BF16).reshape(16, BLOCK, 256)
+
+    def cw(c):
+        for k in range(5):
+            sent(c, X_KIND + k, x_send(c, k)[0])
 
     def sw(c):
         for s in range(2):
@@ -327,7 +327,7 @@
                 sent(c, s * 7 + k, a_send(c, s, k)[0])
             for k in range(8):
                 sent(c, RS_KIND + s * 8 + k, r_move(c, s, k)[0])
-        for k in range(10):
+        for k in range(5, 10):
             sent(c, X_KIND + k, x_send(c, k)[0])
 
     def load(i, size):
@@ -356,8 +356,6 @@
 
     load(0, TILE).start()
     load(1, TILE).start()
-    rows_gap = pltpu.make_async_copy(row_hbm, rg, gsem)
-    rows_gap.start()
     v[depth:, :] = jnp.zeros((v.shape[0] - depth, width), BF16)
     for c in range(chunks):
         ag[c, z, y, :, :depth] = a_ref[c * BLOCK : (c + 1) * BLOCK, :]
@@ -368,7 +366,6 @@
         pl.semaphore_signal(barrier, inc=1, device_id=to, device_id_type=MESH)
     pl.semaphore_wait(barrier, len(peer))
 
-    final = final_ref.shape[-1]
     inner, outer = col * width, (row * 16 + col) * final
     inner_row = inner // 128
     outer_row = jnp.minimum(outer // 128, col_ref.shape[0] - 3)
@@ -378,10 +375,12 @@
         near[:, 1536 + 128 * k : 1664 + 128 * k] = col_ref[pl.ds(outer_row + k, 1), :]
     cg[...] = pltpu.roll(jnp.broadcast_to(near[:, :1536], (8, 1536)), (1536 - (inner - inner_row * 128)) % 1536, 1)
     shifted = pltpu.roll(jnp.broadcast_to(near[:, 1536:], (8, 384)), (384 - (outer - outer_row * 128)) % 384, 1)
-    final_ref[...] = shifted[0:1, :final]
-    rows_gap.wait()
-
-    ops = dict(tv=tv, a0=a0, a1=a1, a2=a2, a3=a3, m1=m1, b1=b1, b2=b2, b3=b3, b4=b4, b5=b5, m2=m2, r1=r1, r2=r2, r3=r3, r4=r4, sw=sw)
+    cf[...] = shifted[:, :256]
+    flat = rc.reshape(16 * chunks * BLOCK, 128)
+    for k in range(row_ref.shape[0]):
+        flat[k * 128 : (k + 1) * 128, :] = jnp.broadcast_to(row_ref[k : k + 1, :], (128, 128)).T
+
+    ops = dict(tv=tv, cw=cw, a0=a0, a1=a1, a2=a2, a3=a3, m1=m1, b1=b1, b2=b2, b3=b3, b4=b4, b5=b5, m2=m2, r1=r1, r2=r2, r3=r3, r4=r4, sw=sw)
 
     def step(t, carry):
         for name, late in PLAN:
@@ -405,34 +404,33 @@
 
     vm = pl.BlockSpec(memory_space=pltpu.VMEM)
     anywhere = pl.BlockSpec(memory_space=pl.ANY)
-    cycle_two, here = pl.pallas_call(
+    updated = pl.pallas_call(
         kernel,
-        out_shape=(
-            jax.ShapeDtypeStruct((final, 16 * rows), F32),
-            jax.ShapeDtypeStruct((1, final), F32),
-        ),
-        in_specs=[vm, anywhere, anywhere, vm],
-        out_specs=(vm, vm),
+        out_shape=jax.ShapeDtypeStruct((final, 16 * rows), BF16),
+        in_specs=[vm, anywhere, vm, vm],
+        out_specs=vm,
         scratch_shapes=[
-            pltpu.SMEM((16 * rows,), F32),
             pltpu.VMEM((1, 1920), F32),
             pltpu.VMEM((8, 1536), F32),
+            pltpu.VMEM((8, 256), F32),
+            pltpu.VMEM((16, chunks, BLOCK, 128), F32),
             pltpu.VMEM((padded, width), BF16),
             pltpu.VMEM((2, TILE, depth), BF16),
             pltpu.VMEM((width, 256), BF16),
             pltpu.VMEM((chunks, 4, 4, BLOCK, padded), BF16),
-            pltpu.VMEM((chunks, 256, width), BF16),
+            pltpu.VMEM((SLOTS, 256, width), BF16),
             pltpu.VMEM((chunks, 128, width), BF16),
             pltpu.VMEM((chunks, 32, width), BF16),
             pltpu.VMEM((chunks, 2, 32, width), BF16),
             pltpu.VMEM((chunks, 256, width), BF16),
-            pltpu.VMEM((2, chunks, 4, 4, WINDOW, 128), BF16),
+            pltpu.VMEM((4, depth // 4, 128), F32),
+            pltpu.VMEM((2, chunks, 4, depth // 4, 128), BF16),
             pltpu.VMEM((2, chunks, 4, WINDOW, 128), BF16),
-            pltpu.VMEM((2, chunks, 2, 4, WINDOW, 128), BF16),
+            pltpu.VMEM((2, chunks, depth // 4, 128), BF16),
+            pltpu.VMEM((2, chunks, 2, depth // 4, 128), BF16),
             pltpu.VMEM((2, chunks, WINDOW, 128), BF16),
             pltpu.VMEM((2, chunks, 2, WINDOW, 128), BF16),
-            pltpu.VMEM((16, chunks, BLOCK, 256), F32),
-            pltpu.SemaphoreType.DMA,
+            pltpu.VMEM((16, chunks, BLOCK, 256), BF16),
             pltpu.SemaphoreType.DMA((2,)),
             pltpu.SemaphoreType.DMA((chunks, KINDS)),
             pltpu.SemaphoreType.DMA((chunks, KINDS)),
@@ -443,8 +441,8 @@
         cost_estimate=pl.CostEstimate(
             flops=4 * 16 * rows * depth * width, bytes_accessed=2 * depth * width, transcendentals=0
         ),
-    )(amplitudes, integrals.T, row_gap, col_gap.reshape(-1, 128))
-    return (cycle_two.T / (row_gap[:, None] + here)).astype(BF16)
+    )(amplitudes, integrals.T, row_gap.reshape(-1, 128), col_gap.reshape(-1, 128))
+    return updated.T
 
 
 def solution(mesh):

time: 142 us -> 138 us (0.972)
  Pallas kernels: 139 us -> 135 us
  other arithmetic: 2.41 us -> 0 us
  local copies, waits for them, and re-layouts: 0.01 us -> 1.97 us
    pallas_call x1, Pallas kernels: 139 us -> 135 us  [on_device(): pl.pallas_call(kernel, out_shape=jax.ShapeDtypeStruct((final, 16 * rows),...]
    convert_element_type x1 -> x0, other arithmetic: 2.41 us -> none  [on_device(): return (cycle_two.T / (row_gap[:, None] + here)).astype(BF16)]
    unnamed x2 -> x1, local copies, waits for them, and re-layouts: 0.01 us -> 1.97 us
where the time goes in v1:
time: 138 us; the launch traced here: 137 us
  Pallas kernels  135 us (98%)
  local copies, waits for them, and re-layouts  1.97 us (1%)
    pallas_call x1, Pallas kernels, on_device(): pl.pallas_call(kernel, out_shape=jax.ShapeDtypeStruct((final, 16 * rows),...  135 us

profile of v1, /device:TPU:0, one launch (start us, length us, event | category | flops | bytes accessed | tf_op | source)
XLA Modules:
  0.0 137.1 jit_solution(10660743014383033197)
XLA Ops:
  0.0 135.2 %shard_map.46 = bf16[180,1792]{1,0:T(8,128)(2,1)} custom-call(bf16[112,2880]{1,0:T(8,128)(2,1)} %a_ref.1, bf16[1440,2880]{1,0:T(8,128)(2,1)} %bitcast.5, f32[14,128]{1,0:T(8,128)} %bitcast.7, f32[180,128]{1,0:T(8,128)} %bitcast.6), custom_call_target="tpu_custom_call" | custom-call | flops 29727129600 | bytes 8294400 | tf_op jit(solution)/shard_map/pallas_call | solution.py:407
  135.2 2.0 %copy.6 = bf16[1792,180]{0,1:T(8,128)(2,1)} copy(bf16[1792,180]{0,1:T(8,128)(2,1)} %bitcast.4) | data formatting | bytes 1290240
